TPU v7x, 32 devices: a whole 2x2x4 slice. The times are simulated.
32 devices in a mesh: feat: 4 (over x, core), work: 8 (over z, y).
Axes of the slice: x: 2, y: 2, z: 4, core: 2. Of those that a mesh axis runs over, the one named last changes fastest.
Arguments:
- momentum: bfloat16 [8, 8192, 1024], P('work', 'feat'), may hold values from -6 to 6
- gradient: bfloat16 [8, 8192, 1024], P('work', 'feat'), may hold values from -6 to 6
- weight: bfloat16 [8192, 1024], P('feat'), may hold values from -3 to 3
- tokens: bfloat16 [8192, 8192], P('work', 'feat'), may hold values from -6 to 6
- select: int32 [8, 64, 8, 4], P('work', 'feat'), may hold values from 0 to 127, as said below
Outputs:
- moment_out: bfloat16 [8, 8192, 1024], P('work', 'feat')
- weight_out: bfloat16 [8192, 1024], P('feat')
- projected: bfloat16 [8192, 1024], P('work', 'feat')
Inputs may be any that keep to these rules, and one draw needn't show every extreme that they name: `select`: for each worker and tile the 4 indices are distinct.
All inputs are finite; a program needn't handle non-finite values.
Results may differ from a plain program's by a relative error of at most 0.015.
Values may be sent and summed in bfloat16 or wider, within the bound.
A program may use at most 128 MiB of HBM per device.

v0:
```python
import math
import jax
import jax.numpy as jnp
from jax import lax
from jax.sharding import PartitionSpec as P

D = 8192
TILE = 128
HIGHEST_PRECISION = lax.Precision.HIGHEST
DECAY = 0.9
RATE = 8.0


def cosine_basis(order):
    freq = jnp.arange(order, dtype=jnp.int32).astype(jnp.float32)[:, None]
    place = jnp.arange(order, dtype=jnp.int32).astype(jnp.float32)[None, :]
    scale = jnp.where(freq == 0.0, math.sqrt(1.0 / order), math.sqrt(2.0 / order))
    return scale * jnp.cos(math.pi * (2.0 * place + 1.0) * freq / (2.0 * order))


def local(momentum, gradient, weight, tokens, select):
    transform = cosine_basis(TILE)
    local_rows, out_width = weight.shape
    row_tiles = local_rows // TILE
    col_tiles = out_width // TILE
    workers = lax.axis_size("work")
    positions = jnp.arange(TILE, dtype=jnp.int32)
    chosen = select[0]
    blended = (DECAY * momentum[0].astype(jnp.float32) + gradient[0].astype(jnp.float32)).reshape(
        row_tiles, TILE, col_tiles, TILE
    )
    onehot = (chosen[..., None] == positions).astype(jnp.float32)
    rows_basis = jnp.einsum("abkr,rj->abkj", onehot, transform, precision=HIGHEST_PRECISION)
    partial_value = jnp.einsum("abkr,arbc->akbc", rows_basis, blended, precision=HIGHEST_PRECISION)
    decoded = jnp.einsum("abkr,akbc->arbc", rows_basis, partial_value, precision=HIGHEST_PRECISION)
    moment_out = (blended - decoded).reshape(local_rows, out_width).astype(jnp.bfloat16)[None]
    row_marks = jnp.arange(TILE, dtype=jnp.int32).astype(jnp.float32)
    initial = jnp.zeros((row_tiles, TILE, col_tiles, TILE), jnp.float32)
    values = lax.all_gather(
        partial_value[None].astype(jnp.bfloat16), "work", axis=0, tiled=True
    ).astype(jnp.float32)
    locations = lax.all_gather(
        chosen.astype(jnp.float32)[None].astype(jnp.bfloat16), "work", axis=0, tiled=True
    ).astype(jnp.float32)
    indicator = (locations[..., None] == row_marks).astype(jnp.float32)
    summed = initial + jnp.einsum(
        "nabkr,nakbc->arbc", indicator, values, precision=HIGHEST_PRECISION
    )
    weight_out = (
        weight.astype(jnp.float32)
        - RATE
        * jnp.einsum(
            "rj,arbc->ajbc", transform, summed / workers, precision=HIGHEST_PRECISION
        ).reshape(local_rows, out_width)
    ).astype(jnp.bfloat16)
    summed_out = lax.psum_scatter(
        lax.dot_general(
            weight_out, tokens, (((0,), (1,)), ((), ())), preferred_element_type=jnp.float32
        ).astype(jnp.bfloat16),
        "feat",
        scatter_dimension=0,
        tiled=True,
    ).astype(jnp.float32)
    projected = (summed_out.T * (1.0 / math.sqrt(D))).astype(jnp.bfloat16)
    return (moment_out, weight_out, projected)


def solution(mesh):
    in_specs = (
        P("work", "feat", None),
        P("work", "feat", None),
        P("feat", None),
        P("work", "feat"),
        P("work", "feat", None, None),
    )
    out_specs = (P("work", "feat", None), P("feat", None), P("work", "feat"))
    return jax.shard_map(local, mesh=mesh, in_specs=in_specs, out_specs=out_specs, check_vma=False)
```

profile of v0, /device:TPU:0, one launch (start us, length us, event | category | flops | bytes accessed | tf_op | source)
XLA Modules:
  0.0 166.0 jit_solution(15831966459224031147)
XLA Ops:
  7.2 0.0 all-gather.3.cloned.1.call-start
  7.2 0.8 copy.35
  8.0 0.1 iota_compare_fusion
  8.2 5.5 %add_bitcast_fusion = f32[256,8,8,128]{3,1,2,0:T(8,128)S(1)} fusion(bf16[1,2048,1024]{2,1,0:T(8,128)(2,1)} %param.6, bf16[1,2048,1024]{2,1,0:T(8,128)(2,1)} %param.5), kind=kLoop, calls=%fused_computation.8 | loop fusion | flops 8388608 | bytes 16777216
  13.7 5.3 %copy.54 = f32[256,8,8,128]{3,2,1,0:T(8,128)} copy(f32[256,8,8,128]{3,1,2,0:T(8,128)S(1)} %add_bitcast_fusion) | data formatting | bytes 16777216
  19.0 9.3 %copy.39 = f32[16,128,8,128]{1,3,2,0:T(8,128)} copy(f32[16,128,8,128]{3,2,1,0:T(8,128)} %bitcast.51) | data formatting | bytes 16777216 | tf_op jit(solution)/shard_map/add | solution.py:29
  28.3 0.6 fusion.11
  28.9 15.4 %fusion.27 = (bf16[16,4,8,128]{3,1,2,0:T(4,128)(2,1)S(1)}, f32[16,4,8,128]{3,1,2,0:T(4,128)S(1)}) fusion(f32[16,128,8,128]{1,3,2,0:T(8,128)} %copy.39, f32[16,8,4,128]{3,2,1,0:T(4,128)S(1)} %fusion.11), kind=kOutput, calls=%fused_computation.40 | convolution fusion | flops 100728832 | bytes 9043968 | tf_op jit(solution)/shard_map/abkr,arbc->akbc/dot_general | solution.py:34
  44.2 0.7 copy.41
  45.0 0.0 reduce-scatter.2.cloned.1.call-start
  45.0 32.6 %all_gather.7 = bf16[8,16,8,4]{1,2,3,0:T(8,128)(2,1)S(1)} all-gather(bf16[1,16,8,4]{1,2,3,0:T(8,128)(2,1)S(1)} %fusion.23), channel_id=1, replica_groups=mesh['feat'=4,'work'=8] {'work'}, dimensions={0}, use_global_device_ids=true | all-gather | bytes 9216 | tf_op jit(solution)/shard_map/all_gather | solution.py:42
  77.7 0.5 copy.43
  78.2 9.9 %all-gather.3.cloned.1.call-done = bf16[128,4,8,128]{3,2,1,0:T(8,128)(2,1)} async-done(((bf16[16,4,8,128]{3,2,1,0:T(8,128)(2,1)}), bf16[128,4,8,128]{3,2,1,0:T(8,128)(2,1)}) %all-gather.3.cloned.1.call-update) | async-done | bytes 1048592 | tf_op jit(solution)/shard_map/all_gather | solution.py:39
  88.1 4.8 %fusion.7 = f32[16,8,128,128,1]{3,2,4,1,0:T(8,128)S(1)} fusion(bf16[8,16,4,8,128]{4,3,2,1,0:T(8,128)(2,1)} %bitcast.54, f32[128]{0:T(128)S(1)} %iota_convert_fusion, f32[8,16,8,4]{3,2,1,0:T(8,128)S(1)} %copy.43), kind=kOutput, calls=%fused_computation.10 | convolution fusion | flops 134742016 | bytes 9454080 | tf_op jit(solution)/shard_map/nabkr,nakbc->arbc/dot_general | solution.py:46
  92.9 9.5 %multiply_bitcast_fusion = f32[16,128,8,128]{1,3,2,0:T(8,128)} fusion(f32[16,8,128,128,1]{3,2,4,1,0:T(8,128)S(1)} %fusion.7, f32[128]{0:T(128)S(1)} %iota_convert_fusion, f32[128]{0:T(128)S(1)} %get-tuple-element.18, f32[128]{0:T(128)S(1)} %get-tuple-element.17), kind=kOutput, calls=%fused_computation.7 | convolution fusion | flops 3225468928 | bytes 16778752 | tf_op jit(solution)/shard_map/rj,arbc->ajbc/dot_general | solution.py:52
  102.4 9.3 %copy.45 = f32[16,128,8,128]{3,2,1,0:T(8,128)} copy(f32[16,128,8,128]{1,3,2,0:T(8,128)} %multiply_bitcast_fusion) | data formatting | bytes 16777216 | tf_op jit(solution)/shard_map/mul | solution.py:51
  111.6 6.9 %fusion = bf16[2048,1024]{1,0:T(8,128)(2,1)S(1)} fusion(f32[256,8,8,128]{3,2,1,0:T(8,128)} %bitcast.52, bf16[2048,1024]{1,0:T(8,128)(2,1)} %param.7), kind=kLoop, calls=%fused_computation.1 | loop fusion | flops 6291456 | bytes 16777216 | tf_op jit(solution)/shard_map/convert_element_type | solution.py:55
  118.6 2.0 %copy-done = bf16[2048,1024]{1,0:T(8,128)(2,1)} copy-done((bf16[2048,1024]{1,0:T(8,128)(2,1)}, bf16[2048,1024]{1,0:T(8,128)(2,1)S(1)}, u32[]{:S(2)}) %copy-start) | copy-done | bytes 4194328
  120.6 5.8 %convolution_convert_fusion = bf16[1024,1024]{1,0:T(8,128)(2,1)} fusion(bf16[2048,1024]{1,0:T(8,128)(2,1)S(1)} %fusion, bf16[1024,2048]{1,0:T(8,128)(2,1)S(1)} %copy-done.2), kind=kOutput, calls=%fused_computation.12 | convolution fusion | flops 4296015872 | bytes 10485760 | tf_op jit(solution)/shard_map/dot_general | solution.py:57
  126.4 16.6 %fusion.3 = bf16[16,128,8,128]{1,3,2,0:T(8,128)(2,1)} fusion(f32[16,128,8,128]{1,3,2,0:T(8,128)} %copy.39, f32[16,4,8,128]{3,1,2,0:T(4,128)S(1)} %get-tuple-element.16, f32[16,8,4,128]{3,2,1,0:T(4,128)S(1)} %fusion.11), kind=kOutput, calls=%fused_computation.6 | convolution fusion | flops 104857600 | bytes 13107200 | tf_op jit(solution)/shard_map/abkr,akbc->arbc/dot_general | solution.py:35
  143.0 6.7 %copy.40 = bf16[16,128,8,128]{3,2,1,0:T(8,128)(2,1)} copy(bf16[16,128,8,128]{1,3,2,0:T(8,128)(2,1)} %fusion.3) | data formatting | bytes 8388608 | tf_op jit(solution)/shard_map/convert_element_type | solution.py:36
  149.7 7.3 %convert_element_type.90 = bf16[1,2048,1024]{2,1,0:T(8,128)(2,1)} reshape(bf16[16,128,8,128]{3,2,1,0:T(8,128)(2,1)} %copy.40) | data formatting | bytes 8388608 | tf_op jit(solution)/shard_map/convert_element_type | solution.py:36
  157.0 1.1 fusion.10
  158.1 1.0 copy.46
  (11 shorter events, 0.1 us)
Async XLA Ops:
  7.2 80.9 %all-gather.3.cloned.1.call-start = ((), (), s32[]{:S(2)}) async-start(), calls=%async_computation.2 | async-start | bytes 1179648 | tf_op jit(solution)/shard_map/all_gather | solution.py:39
  28.3 16.8 %copy-start.1 = (s32[1,16,8,4]{1,3,2,0:T(4,128)S(1)}, s32[1,16,8,4]{1,3,2,0:T(4,128)}, u32[]{:S(2)}) copy-start(s32[1,16,8,4]{1,3,2,0:T(4,128)} %param.9) | copy-start | bytes 6148
  45.0 112.0 %reduce-scatter.2.cloned.1.call-start = ((), (), s32[]{:S(2)}) async-start(), calls=%async_computation.1 | async-start | bytes 2621440 | tf_op jit(solution)/shard_map/reduce_scatter | solution.py:56
  111.6 9.0 %copy-start.2 = (bf16[1024,2048]{1,0:T(8,128)(2,1)S(1)}, bf16[1024,2048]{1,0:T(8,128)(2,1)}, u32[]{:S(2)}) copy-start(bf16[1024,2048]{1,0:T(8,128)(2,1)} %param.8) | copy-start | bytes 12582916
  118.6 2.0 %copy-start = (bf16[2048,1024]{1,0:T(8,128)(2,1)}, bf16[2048,1024]{1,0:T(8,128)(2,1)S(1)}, u32[]{:S(2)}) copy-start(bf16[2048,1024]{1,0:T(8,128)(2,1)S(1)} %fusion) | copy-start | bytes 12582916
Sparse Core Ops, SparseCore 0:
  45.1 42.9 all-gather.2
  126.5 30.2 reduce-scatter.1
where the time goes:
time: 167 us; the launch traced here: 166 us
  matrix products  52.6 us (31%)
  local copies, waits for them, and re-layouts  42.9 us (26%)
  blocking collectives  32.6 us (20%)
  between operations  14.1 us (8%)
  other arithmetic  13.7 us (8%)
  waiting for transfers between devices  9.98 us (6%)
    all_gather x1, blocking collectives, local(): lax.all_gather(chosen.astype(jnp.float32)[None].astype(jnp.bfloat16), 'wo...  32.6 us
    dot_general x1, matrix products, local(): jnp.einsum('abkr,akbc->arbc', rows_basis, partial_value, precision=HIGHES...  16.6 us
    dot_general x1, matrix products, local(): jnp.einsum('abkr,arbc->akbc', rows_basis, blended, precision=HIGHEST_PREC...  15.4 us
    convert_element_type x2, local copies, waits for them, and re-layouts, local(): (blended - decoded).reshape(local_rows, out_width).astype(jnp.bfloat16)  14 us
    all_gather x1, waiting for transfers between devices, local(): lax.all_gather(partial_value[None].astype(jnp.bfloat16), 'work', axis=0,...  9.95 us
    dot_general x1, matrix products, local(): jnp.einsum('rj,arbc->ajbc', transform, summed / workers, precision=HIGHES...  9.49 us
    add x1, local copies, waits for them, and re-layouts, local(): DECAY * momentum[0].astype(jnp.float32) + gradient[0].astype(jnp.float32)  9.29 us
    mul x1, local copies, waits for them, and re-layouts, local(): RATE * jnp.einsum('rj,arbc->ajbc', transform, summed / workers, precision...  9.28 us
  transfers between devices with their start and end apart: 2, of which 1 were waited for; matrix products, arithmetic and copies ran while one was open for 19% of the time, Pallas kernels for 0%

commit v1 on v0

--- a/solution.py
+++ b/solution.py
@@ -9,6 +9,34 @@
 HIGHEST_PRECISION = lax.Precision.HIGHEST
 DECAY = 0.9
 RATE = 8.0
+
+
+def runs_scan(sheet):
+    before, z, outer = (lax.axis_size("work"), lax.axis_index("work"), sheet.shape[0])
+    local_now = lax.dynamic_update_slice_in_dim(
+        jnp.zeros(
+            [j * before if nth == 0 else j for nth, j in enumerate(sheet.shape)], sheet.dtype
+        ),
+        sheet,
+        z * outer,
+        axis=0,
+    )
+    p_next = upper = sheet
+    for k0 in [*range(1, before // 2 + 1)]:
+        p_next = lax.ppermute(
+            p_next, axis_name="work", perm=[(nth, (nth + 1) % before) for nth in range(before)]
+        )
+        local_now = lax.dynamic_update_slice_in_dim(
+            local_now, p_next, (z - k0) % before * outer, axis=0
+        )
+        if 2 * k0 < before:
+            upper = lax.ppermute(
+                upper, axis_name="work", perm=[(nth, (nth - 1) % before) for nth in range(before)]
+            )
+            local_now = lax.dynamic_update_slice_in_dim(
+                local_now, upper, (z + k0) % before * outer, axis=0
+            )
+    return local_now
 
 
 def cosine_basis(order):
@@ -36,9 +64,7 @@
     moment_out = (blended - decoded).reshape(local_rows, out_width).astype(jnp.bfloat16)[None]
     row_marks = jnp.arange(TILE, dtype=jnp.int32).astype(jnp.float32)
     initial = jnp.zeros((row_tiles, TILE, col_tiles, TILE), jnp.float32)
-    values = lax.all_gather(
-        partial_value[None].astype(jnp.bfloat16), "work", axis=0, tiled=True
-    ).astype(jnp.float32)
+    values = runs_scan(partial_value[None].astype(jnp.bfloat16)).astype(jnp.float32)
     locations = lax.all_gather(
         chosen.astype(jnp.float32)[None].astype(jnp.bfloat16), "work", axis=0, tiled=True
     ).astype(jnp.float32)

time: 167 us -> 182 us (1.090)
  starting transfers between devices: 0.08 us -> 15.6 us
  waiting for transfers between devices: 9.98 us -> 13.7 us
  blocking collectives: 32.6 us -> 30.5 us
  matrix products: 52.6 us -> 50.7 us
    ppermute x0 -> x7, starting transfers between devices: none -> 15.6 us  [the longest x3 12.5 us: runs_scan(): lax.ppermute(upper, axis_name='work', perm=[(nth, (nth - 1) % before) for...]
    ppermute x0 -> x7, waiting for transfers between devices: none -> 13.7 us  [the longest x4 13.6 us: runs_scan(): lax.ppermute(p_next, axis_name='work', perm=[(nth, (nth + 1) % before) fo...]
    all_gather x1 -> x0, waiting for transfers between devices: 9.95 us -> none  [local(): lax.all_gather(partial_value[None].astype(jnp.bfloat16), 'work', axis=0,...]
    all_gather x1, blocking collectives: 32.6 us -> 30.5 us  [local(): lax.all_gather(chosen.astype(jnp.float32)[None].astype(jnp.bfloat16), 'wo...]
  transfers between devices with their start and end apart: 2 -> 8, of which waited for: 1 -> 3; matrix products, arithmetic and copies ran while one was open for 19% -> 18% of each run, Pallas kernels for 0% -> 0%
where the time goes in v1:
time: 182 us
  matrix products  50.7 us (28%)
  local copies, waits for them, and re-layouts  43.1 us (24%)
  blocking collectives  30.5 us (17%)
  starting transfers between devices  15.6 us (9%)
  between operations  14.2 us (8%)
  other arithmetic  13.8 us (8%)
  waiting for transfers between devices  13.7 us (8%)
    all_gather x1, blocking collectives, local(): lax.all_gather(chosen.astype(jnp.float32)[None].astype(jnp.bfloat16), 'wo...  30.5 us
    dot_general x1, matrix products, local(): jnp.einsum('abkr,akbc->arbc', rows_basis, partial_value, precision=HIGHES...  16.6 us
    dot_general x1, matrix products, local(): jnp.einsum('abkr,arbc->akbc', rows_basis, blended, precision=HIGHEST_PREC...  15.4 us
    convert_element_type x2, local copies, waits for them, and re-layouts, local(): (blended - decoded).reshape(local_rows, out_width).astype(jnp.bfloat16)  14 us
    ppermute x4, waiting for transfers between devices, runs_scan(): lax.ppermute(p_next, axis_name='work', perm=[(nth, (nth + 1) % before) fo...  13.6 us
    ppermute x3, starting transfers between devices, runs_scan(): lax.ppermute(upper, axis_name='work', perm=[(nth, (nth - 1) % before) for...  12.5 us
    dot_general x1, matrix products, local(): jnp.einsum('rj,arbc->ajbc', transform, summed / workers, precision=HIGHES...  9.41 us
    add x1, local copies, waits for them, and re-layouts, local(): DECAY * momentum[0].astype(jnp.float32) + gradient[0].astype(jnp.float32)  9.28 us
  transfers between devices with their start and end apart: 8, of which 3 were waited for; matrix products, arithmetic and copies ran while one was open for 18% of the time, Pallas kernels for 0%

profile of v1, /device:TPU:0, one launch (start us, length us, event | category | flops | bytes accessed | tf_op | source)
XLA Modules:
  0.0 181.6 jit_solution(4495020270984684807)
XLA Ops:
  7.2 0.8 copy.23
  8.2 5.5 %add_bitcast_fusion = f32[256,8,8,128]{3,1,2,0:T(8,128)S(1)} fusion(bf16[1,2048,1024]{2,1,0:T(8,128)(2,1)} %param.6, bf16[1,2048,1024]{2,1,0:T(8,128)(2,1)} %param.5), kind=kLoop, calls=%fused_computation.9 | loop fusion | flops 8388608 | bytes 16777216
  13.7 5.3 %copy.48 = f32[256,8,8,128]{3,2,1,0:T(8,128)} copy(f32[256,8,8,128]{3,1,2,0:T(8,128)S(1)} %add_bitcast_fusion) | data formatting | bytes 16777216
  19.0 9.3 %copy.27 = f32[16,128,8,128]{1,3,2,0:T(8,128)} copy(f32[16,128,8,128]{3,2,1,0:T(8,128)} %bitcast.50) | data formatting | bytes 16777216 | tf_op jit(solution)/shard_map/add | solution.py:57
  28.9 15.4 %convolution_bitcast_fusion = f32[16,4,8,128]{3,1,2,0:T(4,128)S(1)} fusion(f32[16,128,8,128]{1,3,2,0:T(8,128)} %copy.27, f32[16,8,4,128]{3,2,1,0:T(4,128)S(1)} %fusion.11), kind=kOutput, calls=%fused_computation.13 | convolution fusion | flops 100663296 | bytes 8912896 | tf_op jit(solution)/shard_map/abkr,arbc->akbc/dot_general | solution.py:62
  44.3 3.0 %collective-permute-start = (bf16[1,16,4,8,128]{4,2,3,1,0:T(4,128)(2,1)S(1)}, bf16[1,16,4,8,128]{4,2,3,1,0:T(4,128)(2,1)S(1)}, u32[]{:S(2)}, u32[]{:S(2)}) collective-permute-start(bf16[1,16,4,8,128]{4,2,3,1,0:T(4,128)(2,1)S(1)} %convert_bitcast_fusion), channel_id=1, source_target_pairs={{0,1},{1,2},{2,3},{3,4},{4,5},{5,6},{6,7},{7,0},{8,9},{9,10},{10,1... | collective-permute-start | bytes 393224 | tf_op jit(solution)/shard_map/ppermute | solution.py:26
  47.3 3.1 %collective-permute-start.1 = (bf16[1,16,4,8,128]{4,2,3,1,0:T(4,128)(2,1)S(1)}, bf16[1,16,4,8,128]{4,2,3,1,0:T(4,128)(2,1)S(1)}, u32[]{:S(2)}, u32[]{:S(2)}) collective-permute-start(bf16[1,16,4,8,128]{4,2,3,1,0:T(4,128)(2,1)S(1)} %convert_bitcast_fusion), channel_id=1, source_target_pairs={{0,7},{1,0},{2,1},{3,2},{4,3},{5,4},{6,5},{7,6},{8,15},{9,8},{10,9... | collective-permute-start | bytes 393224 | tf_op jit(solution)/shard_map/ppermute | solution.py:33
  50.4 30.5 %all_gather.3 = bf16[8,16,8,4]{1,2,3,0:T(8,128)(2,1)S(1)} all-gather(bf16[1,16,8,4]{1,2,3,0:T(8,128)(2,1)S(1)} %fusion.23), channel_id=1, replica_groups=mesh['feat'=4,'work'=8] {'work'}, dimensions={0}, use_global_device_ids=true | all-gather | bytes 9216 | tf_op jit(solution)/shard_map/all_gather | solution.py:68
  82.1 4.7 %collective-permute-start.3 = (bf16[1,16,4,8,128]{4,2,3,1,0:T(4,128)(2,1)S(1)}, bf16[1,16,4,8,128]{4,2,3,1,0:T(4,128)(2,1)S(1)}, u32[]{:S(2)}, u32[]{:S(2)}) collective-permute-start(bf16[1,16,4,8,128]{4,2,3,1,0:T(4,128)(2,1)S(1)} %collective-permute-done.1), channel_id=1, source_target_pairs={{0,7},{1,0},{2,1},{3,2},{4,3},{5,4},{6,5},{7,6},{8,15},{9,8},{10,9... | collective-permute-start | bytes 393224 | tf_op jit(solution)/shard_map/ppermute | solution.py:33
  86.9 3.2 %collective-permute-done.2 = bf16[1,16,4,8,128]{4,2,3,1,0:T(4,128)(2,1)S(1)} collective-permute-done((bf16[1,16,4,8,128]{4,2,3,1,0:T(4,128)(2,1)S(1)}, bf16[1,16,4,8,128]{4,2,3,1,0:T(4,128)(2,1)S(1)}, u32[]{:S(2)}, u32[]{:S(2)}) %collective-permute-start.2) | collective-permute-done | bytes 131104 | tf_op jit(solution)/shard_map/ppermute | solution.py:26
  90.1 4.7 %collective-permute-start.5 = (bf16[1,16,4,8,128]{4,2,3,1,0:T(4,128)(2,1)S(1)}, bf16[1,16,4,8,128]{4,2,3,1,0:T(4,128)(2,1)S(1)}, u32[]{:S(2)}, u32[]{:S(2)}) collective-permute-start(bf16[1,16,4,8,128]{4,2,3,1,0:T(4,128)(2,1)S(1)} %collective-permute-done.3), channel_id=1, source_target_pairs={{0,7},{1,0},{2,1},{3,2},{4,3},{5,4},{6,5},{7,6},{8,15},{9,8},{10,9... | collective-permute-start | bytes 393224 | tf_op jit(solution)/shard_map/ppermute | solution.py:33
  95.0 2.9 %collective-permute-done.4 = bf16[1,16,4,8,128]{4,2,3,1,0:T(4,128)(2,1)S(1)} collective-permute-done((bf16[1,16,4,8,128]{4,2,3,1,0:T(4,128)(2,1)S(1)}, bf16[1,16,4,8,128]{4,2,3,1,0:T(4,128)(2,1)S(1)}, u32[]{:S(2)}, u32[]{:S(2)}) %collective-permute-start.4) | collective-permute-done | bytes 131104 | tf_op jit(solution)/shard_map/ppermute | solution.py:26
  98.0 7.5 %collective-permute-done.6 = bf16[1,16,4,8,128]{4,2,3,1,0:T(4,128)(2,1)S(1)} collective-permute-done((bf16[1,16,4,8,128]{4,2,3,1,0:T(4,128)(2,1)S(1)}, bf16[1,16,4,8,128]{4,2,3,1,0:T(4,128)(2,1)S(1)}, u32[]{:S(2)}, u32[]{:S(2)}) %collective-permute-start.6) | collective-permute-done | bytes 131104 | tf_op jit(solution)/shard_map/ppermute | solution.py:26
  105.6 2.9 %fusion.7 = f32[16,8,128,128,1]{3,2,1,0,4:T(8,128)S(1)} fusion(bf16[8,16,4,8,128]{4,2,1,3,0:T(4,128)(2,1)S(1)} %copy_dynamic-update-slice_fusion, f32[128]{0:T(128)S(1)} %iota_convert_fusion, f32[8,16,8,4]{3,1,2,0:T(8,128)S(1)} %copy.38), kind=kOutput, calls=%fused_computation.10 | convolution fusion | flops 134742016 | bytes 9454080 | tf_op jit(solution)/shard_map/nabkr,nakbc->arbc/dot_general | solution.py:72
  108.6 9.4 %multiply_bitcast_fusion = f32[16,128,8,128]{1,3,2,0:T(8,128)} fusion(f32[128]{0:T(128)S(1)} %iota_convert_fusion, f32[128]{0:T(128)S(1)} %get-tuple-element.13, f32[128]{0:T(128)S(1)} %get-tuple-element.12, f32[16,8,128,128,1]{3,2,1,0,4:T(8,128)S(1)} %fusion.7), kind=kOutput, calls=%fused_computation.8 | convolution fusion | flops 3225468928 | bytes 16778752 | tf_op jit(solution)/shard_map/rj,arbc->ajbc/dot_general | solution.py:78
  118.0 9.3 %copy.40 = f32[16,128,8,128]{3,2,1,0:T(8,128)} copy(f32[16,128,8,128]{1,3,2,0:T(8,128)} %multiply_bitcast_fusion) | data formatting | bytes 16777216 | tf_op jit(solution)/shard_map/mul | solution.py:77
  127.2 6.9 %fusion = bf16[2048,1024]{1,0:T(8,128)(2,1)S(1)} fusion(f32[256,8,8,128]{3,2,1,0:T(8,128)} %bitcast.51, bf16[2048,1024]{1,0:T(8,128)(2,1)} %param.7), kind=kLoop, calls=%fused_computation.1 | loop fusion | flops 6291456 | bytes 16777216 | tf_op jit(solution)/shard_map/convert_element_type | solution.py:81
  134.2 2.0 %copy-done = bf16[2048,1024]{1,0:T(8,128)(2,1)} copy-done((bf16[2048,1024]{1,0:T(8,128)(2,1)}, bf16[2048,1024]{1,0:T(8,128)(2,1)S(1)}, u32[]{:S(2)}) %copy-start) | copy-done | bytes 4194328
  136.2 5.8 %convolution_convert_fusion = bf16[1024,1024]{1,0:T(8,128)(2,1)} fusion(bf16[2048,1024]{1,0:T(8,128)(2,1)S(1)} %fusion, bf16[1024,2048]{1,0:T(8,128)(2,1)S(1)} %copy-done.2), kind=kOutput, calls=%fused_computation.12 | convolution fusion | flops 4296015872 | bytes 10485760 | tf_op jit(solution)/shard_map/dot_general | solution.py:83
  142.0 16.6 %fusion.2 = bf16[16,128,8,128]{1,3,2,0:T(8,128)(2,1)} fusion(f32[16,128,8,128]{1,3,2,0:T(8,128)} %copy.27, f32[16,4,8,128]{3,1,2,0:T(4,128)S(1)} %convolution_bitcast_fusion, f32[16,8,4,128]{3,2,1,0:T(4,128)S(1)} %fusion.11), kind=kOutput, calls=%fused_computation.5 | convolution fusion | flops 104857600 | bytes 13107200 | tf_op jit(solution)/shard_map/abkr,akbc->arbc/dot_general | solution.py:63
  158.6 6.7 %copy.28 = bf16[16,128,8,128]{3,2,1,0:T(8,128)(2,1)} copy(bf16[16,128,8,128]{1,3,2,0:T(8,128)(2,1)} %fusion.2) | data formatting | bytes 8388608 | tf_op jit(solution)/shard_map/convert_element_type | solution.py:64
  165.3 7.3 %convert_element_type.90 = bf16[1,2048,1024]{2,1,0:T(8,128)(2,1)} reshape(bf16[16,128,8,128]{3,2,1,0:T(8,128)(2,1)} %copy.28) | data formatting | bytes 8388608 | tf_op jit(solution)/shard_map/convert_element_type | solution.py:64
  172.6 1.1 fusion.10
  173.7 1.0 copy.41
  (31 shorter events, 2.4 us)
Async XLA Ops:
  7.2 165.4 %reduce-scatter.2.cloned.1.call-start = ((), (), s32[]{:S(2)}) async-start(), calls=%async_computation.1 | async-start | bytes 2621440 | tf_op jit(solution)/shard_map/reduce_scatter | solution.py:82
  28.2 22.2 %copy-start.1 = (s32[1,16,8,4]{1,3,2,0:T(4,128)S(1)}, s32[1,16,8,4]{1,3,2,0:T(4,128)}, u32[]{:S(2)}) copy-start(s32[1,16,8,4]{1,3,2,0:T(4,128)} %param.9) | copy-start | bytes 6148
  44.3 37.7 %collective-permute-start = (bf16[1,16,4,8,128]{4,2,3,1,0:T(4,128)(2,1)S(1)}, bf16[1,16,4,8,128]{4,2,3,1,0:T(4,128)(2,1)S(1)}, u32[]{:S(2)}, u32[]{:S(2)}) collective-permute-start(bf16[1,16,4,8,128]{4,2,3,1,0:T(4,128)(2,1)S(1)} %convert_bitcast_fusion), channel_id=1, source_target_pairs={{0,1},{1,2},{2,3},{3,4},{4,5},{5,6},{6,7},{7,0},{8,9},{9,10},{10,1... | collective-permute-start | bytes 393224 | tf_op jit(solution)/shard_map/ppermute | solution.py:26
  47.3 34.7 %collective-permute-start.1 = (bf16[1,16,4,8,128]{4,2,3,1,0:T(4,128)(2,1)S(1)}, bf16[1,16,4,8,128]{4,2,3,1,0:T(4,128)(2,1)S(1)}, u32[]{:S(2)}, u32[]{:S(2)}) collective-permute-start(bf16[1,16,4,8,128]{4,2,3,1,0:T(4,128)(2,1)S(1)} %convert_bitcast_fusion), channel_id=1, source_target_pairs={{0,7},{1,0},{2,1},{3,2},{4,3},{5,4},{6,5},{7,6},{8,15},{9,8},{10,9... | collective-permute-start | bytes 393224 | tf_op jit(solution)/shard_map/ppermute | solution.py:33
  82.0 8.1 %collective-permute-start.2 = (bf16[1,16,4,8,128]{4,2,3,1,0:T(4,128)(2,1)S(1)}, bf16[1,16,4,8,128]{4,2,3,1,0:T(4,128)(2,1)S(1)}, u32[]{:S(2)}, u32[]{:S(2)}) collective-permute-start(bf16[1,16,4,8,128]{4,2,3,1,0:T(4,128)(2,1)S(1)} %collective-permute-done), channel_id=1, source_target_pairs={{0,1},{1,2},{2,3},{3,4},{4,5},{5,6},{6,7},{7,0},{8,9},{9,10},{10,1... | collective-permute-start | bytes 393224 | tf_op jit(solution)/shard_map/ppermute | solution.py:26
  82.1 8.1 %collective-permute-start.3 = (bf16[1,16,4,8,128]{4,2,3,1,0:T(4,128)(2,1)S(1)}, bf16[1,16,4,8,128]{4,2,3,1,0:T(4,128)(2,1)S(1)}, u32[]{:S(2)}, u32[]{:S(2)}) collective-permute-start(bf16[1,16,4,8,128]{4,2,3,1,0:T(4,128)(2,1)S(1)} %collective-permute-done.1), channel_id=1, source_target_pairs={{0,7},{1,0},{2,1},{3,2},{4,3},{5,4},{6,5},{7,6},{8,15},{9,8},{10,9... | collective-permute-start | bytes 393224 | tf_op jit(solution)/shard_map/ppermute | solution.py:33
  90.1 7.8 %collective-permute-start.4 = (bf16[1,16,4,8,128]{4,2,3,1,0:T(4,128)(2,1)S(1)}, bf16[1,16,4,8,128]{4,2,3,1,0:T(4,128)(2,1)S(1)}, u32[]{:S(2)}, u32[]{:S(2)}) collective-permute-start(bf16[1,16,4,8,128]{4,2,3,1,0:T(4,128)(2,1)S(1)} %collective-permute-done.2), channel_id=1, source_target_pairs={{0,1},{1,2},{2,3},{3,4},{4,5},{5,6},{6,7},{7,0},{8,9},{9,10},{10,1... | collective-permute-start | bytes 393224 | tf_op jit(solution)/shard_map/ppermute | solution.py:26
  90.1 7.8 %collective-permute-start.5 = (bf16[1,16,4,8,128]{4,2,3,1,0:T(4,128)(2,1)S(1)}, bf16[1,16,4,8,128]{4,2,3,1,0:T(4,128)(2,1)S(1)}, u32[]{:S(2)}, u32[]{:S(2)}) collective-permute-start(bf16[1,16,4,8,128]{4,2,3,1,0:T(4,128)(2,1)S(1)} %collective-permute-done.3), channel_id=1, source_target_pairs={{0,7},{1,0},{2,1},{3,2},{4,3},{5,4},{6,5},{7,6},{8,15},{9,8},{10,9... | collective-permute-start | bytes 393224 | tf_op jit(solution)/shard_map/ppermute | solution.py:33
  97.9 7.7 %collective-permute-start.6 = (bf16[1,16,4,8,128]{4,2,3,1,0:T(4,128)(2,1)S(1)}, bf16[1,16,4,8,128]{4,2,3,1,0:T(4,128)(2,1)S(1)}, u32[]{:S(2)}, u32[]{:S(2)}) collective-permute-start(bf16[1,16,4,8,128]{4,2,3,1,0:T(4,128)(2,1)S(1)} %collective-permute-done.4), channel_id=1, source_target_pairs={{0,1},{1,2},{2,3},{3,4},{4,5},{5,6},{6,7},{7,0},{8,9},{9,10},{10,1... | collective-permute-start | bytes 393224 | tf_op jit(solution)/shard_map/ppermute | solution.py:26
  127.2 9.0 %copy-start.2 = (bf16[1024,2048]{1,0:T(8,128)(2,1)S(1)}, bf16[1024,2048]{1,0:T(8,128)(2,1)}, u32[]{:S(2)}) copy-start(bf16[1024,2048]{1,0:T(8,128)(2,1)} %param.8) | copy-start | bytes 12582916
  134.2 2.0 %copy-start = (bf16[2048,1024]{1,0:T(8,128)(2,1)}, bf16[2048,1024]{1,0:T(8,128)(2,1)S(1)}, u32[]{:S(2)}) copy-start(bf16[2048,1024]{1,0:T(8,128)(2,1)S(1)} %fusion) | copy-start | bytes 12582916
Sparse Core Ops, SparseCore 0:
  142.1 28.6 reduce-scatter.1
